TPU v7x, 32 devices: a whole 2x2x4 slice. The times are simulated.
32 devices in a mesh: gx: 16 (over z, y, x), gy: 2 (over core).
Axes of the slice: x: 2, y: 2, z: 4, core: 2. Of those that a mesh axis runs over, the one named last changes fastest.
Arguments:
- motion: float32 [3, 32, 96, 256], P(None, 'gx', None, 'gy'), may hold values from -6 to 6
- stress: float32 [6, 32, 96, 256], P(None, 'gx', None, 'gy'), may hold values from -6 to 6
- buoyancy: float32 [32, 96, 256], P('gx', None, 'gy'), may hold values from 0.5 to 1.5
- lame_first: float32 [32, 96, 256], P('gx', None, 'gy'), may hold values from 0.5 to 1.5
- lame_shear: float32 [32, 96, 256], P('gx', None, 'gy'), may hold values from 0.5 to 1.5
- surface: float32 [256, 2048], P('gx', 'gy'), may hold values from -2 to 2
- momentum: float32 [2, 256, 2048], P(None, 'gx', 'gy'), may hold values from -3 to 3
- bathymetry: float32 [256, 2048], P('gx', 'gy'), may hold values from 2 to 4
- wet_mask: int32 [256, 2048], P('gx', 'gy'), may hold values 0 or 1
Outputs:
- final_motion: float32 [3, 32, 96, 256], P(None, 'gx', None, 'gy')
- final_stress: float32 [6, 32, 96, 256], P(None, 'gx', None, 'gy')
- final_surface: float32 [256, 2048], P('gx', 'gy')
- final_momentum: float32 [2, 256, 2048], P(None, 'gx', 'gy')
Inputs may be any that keep to these rules, and one draw needn't show every extreme that they name: `wet_mask`: 1 marks a wet ocean cell, 0 a dry one.
All inputs are finite; a program needn't handle non-finite values. No bound on the sum of `wet_mask` on one device may be relied on, other than what follows from the above.
Results may differ from a plain program's by a relative error of at most 0.0001.
Values sent between devices are 32-bit elements; how exact they have to be, the bound alone decides.
A program may use at most 64 MiB of HBM per device.

v0:
```python
import functools

import jax
import jax.numpy as jnp
from jax import lax
from jax.experimental import pallas as pl
from jax.experimental.pallas import tpu as pltpu
from jax.sharding import PartitionSpec as P

RATIO = 8
STEPS = 4
NSUB = 4
SOLID_STEP = 0.2
WAVE_STEP = 0.1
VISCOSITY = 0.05
UPLIFT_GAIN = 0.25
LOAD_GAIN = 8.0

MESH = pl.DeviceIdType.MESH
F32 = jnp.float32


def kernel(
    nx, ny,
    motion, stress, buoy, lame1, lame2, surf, mom, bath, wetm,
    o_motion, o_stress, o_surf, o_mom,
    S, V, Bu, L1, L2, H, M, N, Wi, W, D, wt, Dx, Dy, Ax, Bx, Ay, By, Fx, Up,
    hb_s, ha_xx, hd_xy, hd_yz, hu_yy,
    hb_vx, ha_v, hd_vy, hu_vx, hu_vz,
    cu, cd, hd_c, hu_c,
    xf, xb, hb_x, ha_x, xsf, xsb, hb_xs, ha_xs,
    ls, lr, tops,
    in_sem, send, recv, csend, crecv, xsend, xrecv, lsend, lrecv,
):
    gx = lax.axis_index("gx")
    gy = lax.axis_index("gy")
    has_b, has_a, has_d, has_u = gx > 0, gx < nx - 1, gy > 0, gy < ny - 1
    ahead = (jnp.minimum(gx + 1, nx - 1), gy)
    behind = (jnp.maximum(gx - 1, 0), gy)
    up = (gx, jnp.minimum(gy + 1, ny - 1))
    down = (gx, jnp.maximum(gy - 1, 0))
    dirs = {
        "f": (ahead, has_a, has_b),
        "b": (behind, has_b, has_a),
        "u": (up, has_u, has_d),
        "d": (down, has_d, has_u),
    }
    zdim = S.shape[2]
    lanes = H.shape[1]
    own = surf.shape[1]
    nt = lanes // 128

    loads = [
        pltpu.make_async_copy(a, b, in_sem.at[i])
        for i, (a, b) in enumerate([
            (wetm, Wi),
            (bath, D.at[pl.ds(0, 16), pl.ds(0, own)]),
            (surf, H.at[pl.ds(0, 16), pl.ds(0, own)]),
            (mom.at[0], M.at[pl.ds(0, 16), pl.ds(0, own)]),
            (mom.at[1], N.at[pl.ds(0, 16), pl.ds(0, own)]),
            (motion, V), (stress, S), (buoy, Bu), (lame1, L1), (lame2, L2),
        ])
    ]
    for c in loads:
        c.start()

    def zero_when_absent(flag, refs):
        @pl.when(jnp.logical_not(flag))
        def _():
            for r in refs:
                r[...] = jnp.zeros(r.shape, F32)

    zero_when_absent(has_b, [hb_s, hb_vx, hb_x, hb_xs])
    zero_when_absent(has_a, [ha_xx, ha_v, ha_x, ha_xs, lr])
    zero_when_absent(has_d, [hd_xy, hd_yz, hd_vy, hd_c])
    zero_when_absent(has_u, [hu_yy, hu_vx, hu_vz, hu_c])
    for r in (cu, cd, xf, xb, xsf, xsb, ls, tops):
        r[...] = jnp.zeros(r.shape, F32)

    barrier = pltpu.get_barrier_semaphore()
    for d in "fbud":
        dev, ok, _ = dirs[d]

        @pl.when(ok)
        def _():
            pl.semaphore_signal(barrier, inc=1, device_id=dev, device_id_type=MESH)

    pl.semaphore_wait(barrier, sum(f.astype(jnp.int32) for f in (has_b, has_a, has_d, has_u)))

    class Msg:
        def __init__(self, d, src, dst, ssem, rsem):
            dev, self.ok, self.inc = dirs[d]
            self.c = pltpu.make_async_remote_copy(
                src_ref=src, dst_ref=dst, send_sem=ssem, recv_sem=rsem,
                device_id=dev, device_id_type=MESH)

        def start(self):
            pl.when(self.ok)(lambda: self.c.start())

        def sent(self):
            pl.when(self.ok)(lambda: self.c.wait_send())

        def got(self):
            pl.when(self.inc)(lambda: self.c.wait_recv())

    count = [0]

    def msg(d, src, dst):
        i = count[0]
        count[0] += 1
        return Msg(d, src, dst, send.at[i], recv.at[i])

    am = [
        msg("f", S.at[pl.ds(3, 2), 1], hb_s),
        msg("b", S.at[0, 0], ha_xx),
        msg("u", S.at[3], hd_xy),
        msg("u", S.at[5], hd_yz),
        msg("d", S.at[1], hu_yy),
    ]
    bm = [
        msg("f", V.at[0, 1], hb_vx),
        msg("b", V.at[pl.ds(1, 2), 0], ha_v),
        msg("u", V.at[1], hd_vy),
        msg("d", V.at[0], hu_vx),
        msg("d", V.at[2], hu_vz),
    ]
    xsm = [msg("f", xsf, hb_xs), msg("b", xsb, ha_xs)]

    def xm(slot):
        return [
            Msg("f", xf.at[slot], hb_x.at[slot], xsend.at[0, slot], xrecv.at[0, slot]),
            Msg("b", xb.at[slot], ha_x.at[slot], xsend.at[1, slot], xrecv.at[1, slot]),
        ]

    def cm(slot):
        return [
            Msg("u", cu.at[slot], hd_c.at[slot], csend.at[0, slot], crecv.at[0, slot]),
            Msg("d", cd.at[slot], hu_c.at[slot], csend.at[1, slot], crecv.at[1, slot]),
        ]

    def lm(slot):
        return Msg("b", ls.at[slot], lr.at[slot], lsend.at[slot], lrecv.at[slot])

    lane = lax.broadcasted_iota(jnp.int32, (zdim, 128), 1)
    zrow = lax.broadcasted_iota(jnp.int32, (zdim, 128), 0)
    lane16 = lax.broadcasted_iota(jnp.int32, (16, 128), 1)
    lane8 = lax.broadcasted_iota(jnp.int32, (8, 128), 1)

    def ym(p, halo):
        return pltpu.roll(jnp.where(lane == 127, halo, p), 1, 1)

    def yp(p, halo):
        return pltpu.roll(jnp.where(lane == 0, halo, p), 127, 1)

    def zm(p):
        return jnp.where(zrow == 0, 0.0, pltpu.roll(p, 1, 0))

    def zp(p):
        return jnp.where(zrow == zdim - 1, 0.0, pltpu.roll(p, zdim - 1, 0))

    def rm(a):
        return pltpu.roll(a, 1, 0)

    def rp(a):
        return pltpu.roll(a, a.shape[0] - 1, 0)

    def cmn(a):
        return pltpu.roll(a, 1, 1)

    def cpl(a):
        return pltpu.roll(a, a.shape[1] - 1, 1)

    def fill_c(slot):
        for i, r in enumerate((H, M, N)):
            cu[slot, 16 * i:16 * i + 16, :] = r[0:16, own - 128:own]
            cd[slot, 16 * i:16 * i + 16, :] = r[0:16, 0:128]
        t = jnp.concatenate([V[2, 0, 0:1, :], V[2, 1, 0:1, :]], axis=0)
        cu[slot, 48:50, :] = t
        cd[slot, 48:50, :] = t
        tops[1:3, 0:128] = t

    def use_c(slot):
        for i, r in enumerate((H, M, N)):
            r[0:16, own:lanes] = jnp.where(
                lane16 < 64, hu_c[slot, 16 * i:16 * i + 16, :], hd_c[slot, 16 * i:16 * i + 16, :])
        t = jnp.where(lane8 < 8, hu_c[slot, 48:56, :], pltpu.roll(hd_c[slot, 48:56, :], 16, 1))
        tops[1:3, 128:256] = t[0:2, :]

    def fill_x(slot):
        for i, r in enumerate((H, M, N)):
            xf[slot, 4 * i:4 * i + 4, :] = r[12:16, :]
            xb[slot, 4 * i:4 * i + 4, :] = r[0:4, :]
        xf[slot, 12:14, 0:256] = tops[1:3, :]

    def start_all(ms):
        for m in ms:
            m.start()

    for c in loads[:6]:
        c.wait()
    W[0:16, 0:own] = Wi[...].astype(F32)
    for i, r in enumerate((W, D)):
        cu[0, 56 + 16 * i:72 + 16 * i, :] = r[0:16, own - 128:own]
        cd[0, 56 + 16 * i:72 + 16 * i, :] = r[0:16, 0:128]
    fill_c(0)
    start_all(cm(0))
    loads[6].wait()
    start_all(am)
    for c in loads[7:]:
        c.wait()
    for m in cm(0):
        m.got()
    use_c(0)
    for i, r in enumerate((W, D)):
        r[0:16, own:lanes] = jnp.where(
            lane16 < 64, hu_c[0, 56 + 16 * i:72 + 16 * i, :], hd_c[0, 56 + 16 * i:72 + 16 * i, :])
    for i, r in enumerate((W, D)):
        xsf[4 * i:4 * i + 4, :] = r[12:16, :]
        xsb[4 * i:4 * i + 4, :] = r[0:4, :]
    xsb[8:12, :] = W[0:4, :] * W[1:5, :]
    fill_x(0)
    start_all(xsm)
    start_all(xm(0))

    def ocean_setup():
        for m in xsm:
            m.got()
        for i, r in enumerate((W, D)):
            r[16:24, :] = jnp.concatenate(
                [ha_xs[4 * i:4 * i + 4, :], hb_xs[4 * i:4 * i + 4, :]], axis=0)
        w = W[...]
        d = D[...]
        fx = w * rp(w)
        Fx[...] = fx
        Fx[16:20, :] = ha_xs[8:12, :]
        fx = Fx[...]
        fy = w * cpl(w)
        wt[...] = WAVE_STEP * w
        Dx[...] = d + rp(d)
        Dy[...] = d + cpl(d)
        Bx[...] = VISCOSITY * fx
        By[...] = VISCOSITY * fy
        Ax[...] = fx * (1.0 - VISCOSITY * (rp(fx) + rm(fx) + cpl(fx) + cmn(fx)))
        Ay[...] = fy * (1.0 - VISCOSITY * (rp(fy) + rm(fy) + cpl(fy) + cmn(fy)))

    def mask_flow():
        fx = Fx[...]
        fy = W[...] * cpl(W[...])
        m, n = M[...], N[...]
        mm, nn = fx * m, fy * n
        dm, dn = m - mm, n - nn
        H[...] = H[...] - wt[...] * ((dm - rm(dm)) + (dn - cmn(dn)))
        M[...] = mm
        N[...] = nn

    def substep(_, carry):
        m, n = M[...], N[...]
        mw, ns = rm(m), cmn(n)
        h = H[...] - wt[...] * ((m - mw) + (n - ns))
        H[...] = h
        he, hn = rp(h), cpl(h)
        M[...] = Ax[...] * m + Bx[...] * (
            ((rp(m) + mw) + (cpl(m) + cmn(m))) - (Dx[...] + h + he) * (he - h))
        N[...] = Ay[...] * n + By[...] * (
            ((rp(n) + rm(n)) + (cpl(n) + ns)) - (Dy[...] + h + hn) * (hn - h))
        return carry

    er = lax.broadcasted_iota(jnp.int32, (128, 128), 0)
    ec = lax.broadcasted_iota(jnp.int32, (128, 128), 1)
    row24 = lax.broadcasted_iota(jnp.int32, (24, 128), 0)

    def lift(slot):
        b = hb_x[slot, 12:14, 0:256]
        tops[0:1, :] = b[1:2, :]
        tops[3:4, :] = b[0:1, :]
        t = tops[:, 0:128]
        tiles = [t] + [pltpu.roll(t, 128 - 16 * q, 1) for q in range(1, nt - 1)]
        tiles.append(tops[:, 128:256])
        spread = jnp.where((ec // RATIO) == er, 1.0, 0.0)
        u = jnp.dot(jnp.concatenate(tiles, axis=0), spread,
                    preferred_element_type=F32, precision=lax.Precision.HIGHEST)
        for q in range(nt):
            r = u[8 * q:8 * q + 8, :]
            e = [jnp.broadcast_to(r[i:i + 1, :], (24, 128)) for i in range(4)]
            full = jnp.where(row24 < 8, e[0], jnp.where(row24 < 16, e[1], jnp.where(row24 < 20, e[2], e[3])))
            at = slice(128 * q, 128 * q + 128)
            Up[:, at] = full
        H[...] = H[...] + UPLIFT_GAIN * W[...] * Up[...]

    def average(slot):
        p = W[0:16, 0:own] * H[0:16, 0:own]
        parts = [p[:, 128 * q:128 * q + 128] for q in range(nt - 1)]
        gather = jnp.where((er // RATIO) == ec, 1.0, 0.0)
        g = jnp.dot(jnp.concatenate(parts, axis=0), gather,
                    preferred_element_type=F32, precision=lax.Precision.HIGHEST)
        a0 = jnp.zeros((1, 128), F32)
        a1 = jnp.zeros((1, 128), F32)
        for q in range(nt - 1):
            s0 = jnp.sum(g[16 * q:16 * q + 8, :], axis=0, keepdims=True)
            s1 = jnp.sum(g[16 * q + 8:16 * q + 16, :], axis=0, keepdims=True)
            two = jnp.concatenate([s0, s1, jnp.zeros((6, 128), F32)], axis=0)
            if q:
                two = pltpu.roll(two, 16 * q, 1)
            a0 = a0 + two[0:1, :]
            a1 = a1 + two[1:2, :]
        scale = -LOAD_GAIN / (RATIO * RATIO)
        ls[slot, 0:1, :] = a0 * scale
        ls[slot, 1:2, :] = a1 * scale

    def apply_load(slot):
        lm(slot).got()
        S[2, 0, 0:1, :] = ls[slot, 1:2, :]
        S[2, 1, 0:1, :] = lr[slot, 0:1, :]

    def step(k, carry):
        slot = lax.rem(k, 2)
        nslot = lax.rem(k + 1, 2)
        for m in am:
            m.got()

        @pl.when(k > 0)
        def _():
            apply_load(nslot)

        for x in range(2):
            sb = SOLID_STEP * Bu[x]
            xx, yy, zz, xy, xz, yz = (S[c, x] for c in range(6))
            xx_a = S[0, 1] if x == 0 else ha_xx[...]
            xy_b = hb_s[0] if x == 0 else S[3, 0]
            xz_b = hb_s[1] if x == 0 else S[4, 0]
            V[0, x] = V[0, x] + sb * ((xx_a - xx) + (xy - ym(xy, hd_xy[x])) + (xz - zm(xz)))
            V[1, x] = V[1, x] + sb * ((xy - xy_b) + (yp(yy, hu_yy[x]) - yy) + (yz - zm(yz)))
            V[2, x] = V[2, x] + sb * ((xz - xz_b) + (yz - ym(yz, hd_yz[x])) + (zp(zz) - zz))
        start_all(bm)

        xms = xm(slot)
        for m in xms:
            m.got()
        for i, r in enumerate((H, M, N)):
            r[16:24, :] = jnp.concatenate(
                [ha_x[slot, 4 * i:4 * i + 4, :], hb_x[slot, 4 * i:4 * i + 4, :]], axis=0)

        @pl.when(k == 0)
        def _():
            ocean_setup()
            mask_flow()

        lift(slot)
        lax.fori_loop(0, NSUB, substep, 0)
        average(slot)
        lm(slot).start()

        for m in cm(slot):
            m.sent()

        @pl.when(k < STEPS - 1)
        def _():
            fill_c(nslot)
            start_all(cm(nslot))

        for m in am:
            m.sent()
        for m in bm:
            m.got()
        for x in range(2):
            vx, vy, vz = V[0, x], V[1, x], V[2, x]
            vx_b = hb_vx[...] if x == 0 else V[0, 0]
            vy_a = V[1, 1] if x == 0 else ha_v[0]
            vz_a = V[2, 1] if x == 0 else ha_v[1]
            ex = vx - vx_b
            ey = vy - ym(vy, hd_vy[x])
            ez = vz - zm(vz)
            l, g = SOLID_STEP * L1[x], SOLID_STEP * L2[x]
            tr = l * (ex + ey + ez)
            g2 = 2.0 * g
            S[0, x] = S[0, x] + (tr + g2 * ex)
            S[1, x] = S[1, x] + (tr + g2 * ey)
            S[2, x] = S[2, x] + (tr + g2 * ez)
            S[3, x] = S[3, x] + g * ((yp(vx, hu_vx[x]) - vx) + (vy_a - vy))
            S[4, x] = S[4, x] + g * ((zp(vx) - vx) + (vz_a - vz))
            S[5, x] = S[5, x] + g * ((zp(vy) - vy) + (yp(vz, hu_vz[x]) - vz))

        @pl.when(k < STEPS - 1)
        def _():
            start_all(am)
            for m in cm(nslot):
                m.got()
            use_c(nslot)
            fill_x(nslot)
            start_all(xm(nslot))

        for m in bm:
            m.sent()
        for m in xms:
            m.sent()
        lm(slot).sent()
        return carry

    lax.fori_loop(0, STEPS, step, 0)
    for m in xsm:
        m.sent()
    apply_load((STEPS - 1) % 2)
    outs = [
        pltpu.make_async_copy(a, b, in_sem.at[i])
        for i, (a, b) in enumerate([
            (V, o_motion), (S, o_stress),
            (H.at[pl.ds(0, 16), pl.ds(0, own)], o_surf),
            (M.at[pl.ds(0, 16), pl.ds(0, own)], o_mom.at[0]),
            (N.at[pl.ds(0, 16), pl.ds(0, own)], o_mom.at[1]),
        ])
    ]
    for c in outs:
        c.start()
    for c in outs:
        c.wait()


def body(nx, ny, motion, stress, buoyancy, lame_first, lame_shear, surface, momentum, bathymetry, wet_mask):
    plane = motion.shape[2:]
    two = motion.shape[1:]
    ext = (24, surface.shape[1] + 128)

    def v(*shape):
        return pltpu.VMEM(shape, F32)

    scratch = [v(*stress.shape), v(*motion.shape)] + [v(*two)] * 3
    scratch += [v(*ext)] * 3 + [pltpu.VMEM(wet_mask.shape, jnp.int32)] + [v(*ext)] * 11
    scratch += [v(2, *plane), v(*plane), v(*two), v(*two), v(*two)]
    scratch += [v(*plane), v(2, *plane), v(*two), v(*two), v(*two)]
    scratch += [v(2, 88, 128)] * 4
    scratch += [v(2, 16, ext[1])] * 4 + [v(16, ext[1])] * 4
    scratch += [v(2, 8, 128), v(2, 8, 128), v(8, 256)]
    dma = pltpu.SemaphoreType.DMA
    scratch += [dma((10,)), dma((12,)), dma((12,)), dma((2, 2)), dma((2, 2)), dma((2, 2)), dma((2, 2)), dma((2,)), dma((2,))]
    any_ = pl.BlockSpec(memory_space=pl.ANY)
    return pl.pallas_call(
        functools.partial(kernel, nx, ny),
        out_shape=[
            jax.ShapeDtypeStruct(a.shape, F32) for a in (motion, stress, surface, momentum)
        ],
        in_specs=[any_] * 9,
        out_specs=[any_] * 4,
        scratch_shapes=scratch,
        compiler_params=pltpu.CompilerParams(
            collective_id=0, has_side_effects=True, vmem_limit_bytes=32 * 1024 * 1024
        ),
        name="coupled",
    )(motion, stress, buoyancy, lame_first, lame_shear, surface, momentum, bathymetry, wet_mask)


def solution(mesh):
    return jax.shard_map(
        functools.partial(body, mesh.shape["gx"], mesh.shape["gy"]),
        mesh=mesh,
        in_specs=(
            P(None, "gx", None, "gy"),
            P(None, "gx", None, "gy"),
            P("gx", None, "gy"),
            P("gx", None, "gy"),
            P("gx", None, "gy"),
            P("gx", "gy"),
            P(None, "gx", "gy"),
            P("gx", "gy"),
            P("gx", "gy"),
        ),
        out_specs=(
            P(None, "gx", None, "gy"),
            P(None, "gx", None, "gy"),
            P("gx", "gy"),
            P(None, "gx", "gy"),
        ),
        check_vma=False,
    )
```

profile of v0, /device:TPU:0, one launch (start us, length us, event | category | flops | bytes accessed | tf_op | source)
XLA Modules:
  0.0 69.5 jit_solution(15968067460418148933)
XLA Ops:
  0.6 0.0 copy-start
  0.6 1.1 %copy-done = f32[6,2,96,128]{3,2,1,0:T(8,128)S(1)} copy-done((f32[6,2,96,128]{3,2,1,0:T(8,128)S(1)}, f32[6,2,96,128]{3,2,1,0:T(8,128)}, u32[]{:S(2)}) %copy-start) | copy-done | bytes 589848
  1.7 0.0 copy-start.1
  1.7 1.0 %copy-done.1 = f32[3,2,96,128]{3,2,1,0:T(8,128)S(1)} copy-done((f32[3,2,96,128]{3,2,1,0:T(8,128)S(1)}, f32[3,2,96,128]{3,2,1,0:T(8,128)}, u32[]{:S(2)}) %copy-start.1) | copy-done | bytes 294936
  2.7 0.0 copy-start.2
  2.7 0.9 %copy-done.2 = f32[2,16,1024]{2,1,0:T(8,128)S(1)} copy-done((f32[2,16,1024]{2,1,0:T(8,128)S(1)}, f32[2,16,1024]{2,1,0:T(8,128)}, u32[]{:S(2)}) %copy-start.2) | copy-done | bytes 131096
  3.6 0.0 copy-start.3
  3.6 0.9 %copy-done.3 = f32[2,96,128]{2,1,0:T(8,128)S(1)} copy-done((f32[2,96,128]{2,1,0:T(8,128)S(1)}, f32[2,96,128]{2,1,0:T(8,128)}, u32[]{:S(2)}) %copy-start.3) | copy-done | bytes 98328
  4.5 0.0 copy-start.4
  4.5 0.9 %copy-done.4 = f32[2,96,128]{2,1,0:T(8,128)S(1)} copy-done((f32[2,96,128]{2,1,0:T(8,128)S(1)}, f32[2,96,128]{2,1,0:T(8,128)}, u32[]{:S(2)}) %copy-start.4) | copy-done | bytes 98328
  5.4 0.0 copy-start.5
  5.4 0.9 %copy-done.5 = f32[2,96,128]{2,1,0:T(8,128)S(1)} copy-done((f32[2,96,128]{2,1,0:T(8,128)S(1)}, f32[2,96,128]{2,1,0:T(8,128)}, u32[]{:S(2)}) %copy-start.5) | copy-done | bytes 98328
  6.2 0.0 copy-start.6
  6.2 0.8 %copy-done.6 = f32[16,1024]{1,0:T(8,128)S(1)} copy-done((f32[16,1024]{1,0:T(8,128)S(1)}, f32[16,1024]{1,0:T(8,128)}, u32[]{:S(2)}) %copy-start.6) | copy-done | bytes 65560
  7.1 0.0 copy-start.7
  7.1 0.8 %copy-done.7 = f32[16,1024]{1,0:T(8,128)S(1)} copy-done((f32[16,1024]{1,0:T(8,128)S(1)}, f32[16,1024]{1,0:T(8,128)}, u32[]{:S(2)}) %copy-start.7) | copy-done | bytes 65560
  7.9 0.0 copy-start.8
  7.9 0.8 %copy-done.8 = s32[16,1024]{1,0:T(8,128)S(1)} copy-done((s32[16,1024]{1,0:T(8,128)S(1)}, s32[16,1024]{1,0:T(8,128)}, u32[]{:S(2)}) %copy-start.8) | copy-done | bytes 65560
  8.8 57.9 %coupled.1 = (f32[3,2,96,128]{3,2,1,0:T(8,128)S(1)}, f32[6,2,96,128]{3,2,1,0:T(8,128)S(1)}, f32[16,1024]{1,0:T(8,128)S(1)}, f32[2,16,1024]{2,1,0:T(8,128)S(1)}) custom-call(f32[3,2,96,128]{3,2,1,0:T(8,128)S(1)} %copy-done.1, f32[6,2,96,128]{3,2,1,0:T(8,128)S(1)} %copy-done, f32[2,96,128]{2,1,0:T(8,128)S(1)} %copy-done.3, f32[2,96,128]{2,1,0:T(8,128)S(1)} %copy-done.4, ...), custom_call_target="tpu_custom_call" | custom-call | tf_op jit(solution)/shard_map/coupled/pallas_call | solution.py:436
  66.6 0.7 %copy.17 = f32[3,2,96,128]{3,2,1,0:T(8,128)} copy(f32[3,2,96,128]{3,2,1,0:T(8,128)S(1)} %get-tuple-element.8) | data formatting | bytes 589824
  67.4 0.8 %copy.18 = f32[6,2,96,128]{3,2,1,0:T(8,128)} copy(f32[6,2,96,128]{3,2,1,0:T(8,128)S(1)} %get-tuple-element.9) | data formatting | bytes 1179648
  68.2 0.6 copy.19
  68.8 0.7 copy.20
Async XLA Ops:
  0.6 1.1 %copy-start = (f32[6,2,96,128]{3,2,1,0:T(8,128)S(1)}, f32[6,2,96,128]{3,2,1,0:T(8,128)}, u32[]{:S(2)}) copy-start(f32[6,2,96,128]{3,2,1,0:T(8,128)} %stress.1) | copy-start | bytes 1769476
  1.7 1.0 %copy-start.1 = (f32[3,2,96,128]{3,2,1,0:T(8,128)S(1)}, f32[3,2,96,128]{3,2,1,0:T(8,128)}, u32[]{:S(2)}) copy-start(f32[3,2,96,128]{3,2,1,0:T(8,128)} %motion.1) | copy-start | bytes 884740
  2.7 0.9 %copy-start.2 = (f32[2,16,1024]{2,1,0:T(8,128)S(1)}, f32[2,16,1024]{2,1,0:T(8,128)}, u32[]{:S(2)}) copy-start(f32[2,16,1024]{2,1,0:T(8,128)} %mom.1) | copy-start | bytes 393220
  3.6 0.9 %copy-start.3 = (f32[2,96,128]{2,1,0:T(8,128)S(1)}, f32[2,96,128]{2,1,0:T(8,128)}, u32[]{:S(2)}) copy-start(f32[2,96,128]{2,1,0:T(8,128)} %buoy.1) | copy-start | bytes 294916
  4.5 0.9 %copy-start.4 = (f32[2,96,128]{2,1,0:T(8,128)S(1)}, f32[2,96,128]{2,1,0:T(8,128)}, u32[]{:S(2)}) copy-start(f32[2,96,128]{2,1,0:T(8,128)} %lame1.1) | copy-start | bytes 294916
  5.4 0.9 %copy-start.5 = (f32[2,96,128]{2,1,0:T(8,128)S(1)}, f32[2,96,128]{2,1,0:T(8,128)}, u32[]{:S(2)}) copy-start(f32[2,96,128]{2,1,0:T(8,128)} %lame2.1) | copy-start | bytes 294916
  6.2 0.8 %copy-start.6 = (f32[16,1024]{1,0:T(8,128)S(1)}, f32[16,1024]{1,0:T(8,128)}, u32[]{:S(2)}) copy-start(f32[16,1024]{1,0:T(8,128)} %surf.1) | copy-start | bytes 196612
  7.1 0.8 %copy-start.7 = (f32[16,1024]{1,0:T(8,128)S(1)}, f32[16,1024]{1,0:T(8,128)}, u32[]{:S(2)}) copy-start(f32[16,1024]{1,0:T(8,128)} %bath.1) | copy-start | bytes 196612
  7.9 0.8 %copy-start.8 = (s32[16,1024]{1,0:T(8,128)S(1)}, s32[16,1024]{1,0:T(8,128)}, u32[]{:S(2)}) copy-start(s32[16,1024]{1,0:T(8,128)} %wetm.1) | copy-start | bytes 196612
where the time goes:
time: 69.9 us; the launch traced here: 69.5 us
  Pallas kernels  57.9 us (83%)
  local copies, waits for them, and re-layouts  10.9 us (16%)
    pallas_call x1, Pallas kernels, body(): pl.pallas_call(functools.partial(kernel, nx, ny), out_shape=[jax.ShapeDty...  57.9 us
    unnamed x22, local copies, waits for them, and re-layouts  10.9 us

commit v1 on v0

v1 whole, which is shorter than its diff:
```python
import functools

import jax
import jax.numpy as jnp
from jax import lax
from jax.experimental import pallas as pl
from jax.experimental.pallas import tpu as pltpu
from jax.sharding import PartitionSpec as P

RATIO = 8
STEPS = 4
NSUB = 4
PARTS = 2
SOLID_STEP = 0.2
WAVE_STEP = 0.1
VISCOSITY = 0.05
UPLIFT_GAIN = 0.25
LOAD_GAIN = 8.0

MESH = pl.DeviceIdType.MESH
F32 = jnp.float32


def kernel(
    nx, ny,
    motion, stress, buoy, lame1, lame2, surf, mom, bath, wetm,
    o_motion, o_stress, o_surf, o_mom,
    S, V, Bu, L1, L2, H, M, N, Wi, W, D, wt, Dx, Dy, Ax, Bx, Ay, By, Fx, Up,
    hb_s, ha_xx, hd_s, hu_yy,
    hb_vx, ha_v, hd_vy, hu_v,
    cu, cd, hd_c, hu_c, csu, csd, hd_cs, hu_cs,
    xf, xb, hb_x, ha_x, xsf, xsb, hb_xs, ha_xs,
    ls, lr, tops,
    in_sem, send, recv, csend, crecv, xsend, xrecv, lsend, lrecv,
):
    gx = lax.axis_index("gx")
    gy = lax.axis_index("gy")
    has_b, has_a, has_d, has_u = gx > 0, gx < nx - 1, gy > 0, gy < ny - 1
    ahead = (jnp.minimum(gx + 1, nx - 1), gy)
    behind = (jnp.maximum(gx - 1, 0), gy)
    up = (gx, jnp.minimum(gy + 1, ny - 1))
    down = (gx, jnp.maximum(gy - 1, 0))
    dirs = {
        "f": (ahead, has_a, has_b),
        "b": (behind, has_b, has_a),
        "u": (up, has_u, has_d),
        "d": (down, has_d, has_u),
    }
    zdim = S.shape[2]
    lanes = H.shape[1]
    own = surf.shape[1]
    nt = lanes // 128

    loads = [
        pltpu.make_async_copy(a, b, in_sem.at[i])
        for i, (a, b) in enumerate([
            (wetm, Wi),
            (bath, D.at[pl.ds(0, 16), pl.ds(0, own)]),
            (surf, H.at[pl.ds(0, 16), pl.ds(0, own)]),
            (mom.at[0], M.at[pl.ds(0, 16), pl.ds(0, own)]),
            (mom.at[1], N.at[pl.ds(0, 16), pl.ds(0, own)]),
            (motion.at[pl.ds(1, 2)], V.at[pl.ds(0, 2)]), (motion.at[0], V.at[2]),
            (stress.at[pl.ds(0, 3)], S.at[pl.ds(0, 3)]), (stress.at[3], S.at[4]),
            (stress.at[4], S.at[3]), (stress.at[5], S.at[5]),
            (buoy, Bu), (lame1, L1), (lame2, L2),
        ])
    ]
    for c in loads:
        c.start()

    def zero_when_absent(flag, refs):
        @pl.when(jnp.logical_not(flag))
        def _():
            for r in refs:
                r[...] = jnp.zeros(r.shape, F32)

    zero_when_absent(has_b, [hb_s, hb_vx, hb_x, hb_xs])
    zero_when_absent(has_a, [ha_xx, ha_v, ha_x, ha_xs, lr])
    zero_when_absent(has_d, [hd_s, hd_vy, hd_c, hd_cs])
    zero_when_absent(has_u, [hu_yy, hu_v, hu_c, hu_cs])
    for r in (xf, xb, xsf, xsb, ls, tops):
        r[...] = jnp.zeros(r.shape, F32)

    barrier = pltpu.get_barrier_semaphore()
    for d in "fbud":
        dev, ok, _ = dirs[d]

        @pl.when(ok)
        def _():
            pl.semaphore_signal(barrier, inc=1, device_id=dev, device_id_type=MESH)

    pl.semaphore_wait(barrier, sum(f.astype(jnp.int32) for f in (has_b, has_a, has_d, has_u)))

    class Msg:
        def __init__(self, d, src, dst, ssem, rsem):
            dev, self.ok, self.inc = dirs[d]
            self.c = pltpu.make_async_remote_copy(
                src_ref=src, dst_ref=dst, send_sem=ssem, recv_sem=rsem,
                device_id=dev, device_id_type=MESH)

        def start(self):
            pl.when(self.ok)(lambda: self.c.start())

        def sent(self):
            pl.when(self.ok)(lambda: self.c.wait_send())

        def got(self):
            pl.when(self.inc)(lambda: self.c.wait_recv())

    count = [0]

    def msg(d, src, dst):
        i = count[0]
        count[0] += 1
        return Msg(d, src, dst, send.at[i], recv.at[i])

    size = zdim // PARTS
    am, bm = [], []
    for p in range(PARTS):
        zs = pl.ds(p * size, size)
        am.append([
            msg("f", S.at[pl.ds(3, 2), 1, zs], hb_s.at[:, zs]),
            msg("b", S.at[0, 0, zs], ha_xx.at[zs]),
            msg("u", S.at[pl.ds(4, 2), :, zs], hd_s.at[:, :, zs]),
            msg("d", S.at[1, :, zs], hu_yy.at[:, zs]),
        ])
        bm.append([
            msg("f", V.at[2, 1, zs], hb_vx.at[zs]),
            msg("b", V.at[pl.ds(0, 2), 0, zs], ha_v.at[:, zs]),
            msg("u", V.at[0, :, zs], hd_vy.at[:, zs]),
            msg("d", V.at[pl.ds(1, 2), :, zs], hu_v.at[:, :, zs]),
        ])
    csm = [msg("u", csu, hd_cs), msg("d", csd, hu_cs)]
    xsm = [msg("f", xsf, hb_xs), msg("b", xsb, ha_xs)]

    def xm(slot):
        return [
            Msg("f", xf.at[slot], hb_x.at[slot], xsend.at[0, slot], xrecv.at[0, slot]),
            Msg("b", xb.at[slot], ha_x.at[slot], xsend.at[1, slot], xrecv.at[1, slot]),
        ]

    def cm(slot):
        return [
            Msg("u", cu.at[slot], hd_c.at[slot], csend.at[0, slot], crecv.at[0, slot]),
            Msg("d", cd.at[slot], hu_c.at[slot], csend.at[1, slot], crecv.at[1, slot]),
        ]

    def lm(slot):
        return Msg("b", ls.at[slot], lr.at[slot], lsend.at[slot], lrecv.at[slot])

    lane = lax.broadcasted_iota(jnp.int32, (size, 128), 1)
    zrow = lax.broadcasted_iota(jnp.int32, (size, 128), 0)
    lane24 = lax.broadcasted_iota(jnp.int32, (24, 128), 1)
    lane8 = lax.broadcasted_iota(jnp.int32, (8, 128), 1)

    def ym(p, halo):
        return pltpu.roll(jnp.where(lane == 127, halo, p), 1, 1)

    def yp(p, halo):
        return pltpu.roll(jnp.where(lane == 0, halo, p), 127, 1)

    def zm(ref, c, x, z):
        if z == 0:
            return jnp.where(zrow == 0, 0.0, pltpu.roll(ref[c, x, 0:size, :], 1, 0))
        return pltpu.roll(ref[c, x, z - 8:z + size, :], 1, 0)[8:]

    def zp(ref, c, x, z):
        if z + size == zdim:
            return jnp.where(zrow == size - 1, 0.0, pltpu.roll(ref[c, x, z:zdim, :], size - 1, 0))
        return pltpu.roll(ref[c, x, z:z + size + 8, :], size + 7, 0)[:size]

    def rm(a):
        return pltpu.roll(a, 1, 0)

    def rp(a):
        return pltpu.roll(a, a.shape[0] - 1, 0)

    def cmn(a):
        return pltpu.roll(a, 1, 1)

    def cpl(a):
        return pltpu.roll(a, a.shape[1] - 1, 1)

    half = own // 2

    def fill_x(slot):
        for buf, rows in ((xf, slice(12, 16)), (xb, slice(0, 4))):
            buf[slot, 0:4, 0:own] = H[rows, 0:own]
            buf[slot, 4:8, 0:own] = M[rows, 0:own]
            buf[slot, 0:4, own:own + half] = N[rows, 0:half]
            buf[slot, 4:8, own:own + half] = N[rows, half:own]
        t = jnp.concatenate([V[1, 0, 0:1, :], V[1, 1, 0:1, :]], axis=0)
        xf[slot, 0:2, own + half:own + half + 128] = t
        tops[1:3, 0:128] = t

    def use_x(slot):
        at, left, right = slice(0, own), slice(0, half), slice(half, own)
        n = slice(own, own + half)
        a, b = ha_x, hb_x
        H[16:24, at] = jnp.concatenate([a[slot, 0:4, at], b[slot, 0:4, at]], axis=0)
        M[16:24, at] = jnp.concatenate([a[slot, 4:8, at], b[slot, 4:8, at]], axis=0)
        N[16:24, left] = jnp.concatenate([a[slot, 0:4, n], b[slot, 0:4, n]], axis=0)
        N[16:24, right] = jnp.concatenate([a[slot, 4:8, n], b[slot, 4:8, n]], axis=0)
        t = b[slot, 0:2, own + half:own + half + 128]
        tops[0:1, 0:128] = t[1:2, :]
        tops[3:4, 0:128] = t[0:1, :]

    def fill_c(slot):
        for i, r in enumerate((H, M, N)):
            cu[slot, 24 * i:24 * i + 24, :] = r[:, own - 128:own]
            cd[slot, 24 * i:24 * i + 24, :] = r[:, 0:128]
        cu[slot, 72:80, :] = tops[:, 0:128]
        cd[slot, 72:80, :] = tops[:, 0:128]

    def use_c(slot):
        for i, r in enumerate((H, M, N)):
            at = slice(24 * i, 24 * i + 24)
            r[:, own:lanes] = jnp.where(lane24 < 64, hu_c[slot, at, :], hd_c[slot, at, :])
        tops[:, 128:256] = jnp.where(
            lane8 < 8, hu_c[slot, 72:80, :], pltpu.roll(hd_c[slot, 72:80, :], 16, 1))

    def start_all(ms):
        for m in ms:
            m.start()

    for c in loads[7:11]:
        c.wait()
    for p in range(PARTS):
        start_all(am[p])
    for c in loads[:7]:
        c.wait()
    W[0:16, 0:own] = Wi[...].astype(F32)
    for buf, rows in ((xsf, slice(12, 16)), (xsb, slice(0, 4))):
        buf[0:4, 0:own] = W[rows, 0:own]
        buf[4:8, 0:own] = D[rows, 0:own]
    for q in range(own // 128):
        xsb[q:q + 1, own:own + 128] = W[4:5, 128 * q:128 * q + 128]
    fill_x(0)
    start_all(xm(0))
    start_all(xsm)
    for c in loads[11:]:
        c.wait()

    def bed_x():
        at = slice(0, own)
        W[16:24, at] = jnp.concatenate([ha_xs[0:4, at], hb_xs[0:4, at]], axis=0)
        D[16:24, at] = jnp.concatenate([ha_xs[4:8, at], hb_xs[4:8, at]], axis=0)
        w = W[:, at]
        Fx[:, at] = w * rp(w)
        nextw = jnp.concatenate(
            [ha_xs[q:q + 1, own:own + 128] for q in range(own // 128)], axis=1)
        Fx[16:20, at] = W[16:20, at] * jnp.concatenate([W[17:20, at], nextw], axis=0)
        for i, r in enumerate((W, D, Fx)):
            csu[24 * i:24 * i + 24, :] = r[:, own - 128:own]
            csd[24 * i:24 * i + 24, :] = r[:, 0:128]

    def ocean_setup():
        for i, r in enumerate((W, D, Fx)):
            at = slice(24 * i, 24 * i + 24)
            r[:, own:lanes] = jnp.where(lane24 < 64, hu_cs[at, :], hd_cs[at, :])
        w = W[...]
        d = D[...]
        fx = Fx[...]
        fy = w * cpl(w)
        wt[...] = WAVE_STEP * w
        Dx[...] = d + rp(d)
        Dy[...] = d + cpl(d)
        Bx[...] = VISCOSITY * fx
        By[...] = VISCOSITY * fy
        Ax[...] = fx * (1.0 - VISCOSITY * (rp(fx) + rm(fx) + cpl(fx) + cmn(fx)))
        Ay[...] = fy * (1.0 - VISCOSITY * (rp(fy) + rm(fy) + cpl(fy) + cmn(fy)))

    def mask_flow():
        fx = Fx[...]
        fy = W[...] * cpl(W[...])
        m, n = M[...], N[...]
        mm, nn = fx * m, fy * n
        dm, dn = m - mm, n - nn
        H[...] = H[...] - wt[...] * ((dm - rm(dm)) + (dn - cmn(dn)))
        M[...] = mm
        N[...] = nn

    def substep(_, carry):
        m, n = M[...], N[...]
        mw, ns = rm(m), cmn(n)
        h = H[...] - wt[...] * ((m - mw) + (n - ns))
        H[...] = h
        he, hn = rp(h), cpl(h)
        M[...] = Ax[...] * m + Bx[...] * (
            ((rp(m) + mw) + (cpl(m) + cmn(m))) - (Dx[...] + h + he) * (he - h))
        N[...] = Ay[...] * n + By[...] * (
            ((rp(n) + rm(n)) + (cpl(n) + ns)) - (Dy[...] + h + hn) * (hn - h))
        return carry

    er = lax.broadcasted_iota(jnp.int32, (128, 128), 0)
    ec = lax.broadcasted_iota(jnp.int32, (128, 128), 1)
    row24 = lax.broadcasted_iota(jnp.int32, (24, 128), 0)

    def lift():
        t = tops[:, 0:128]
        tiles = [t] + [pltpu.roll(t, 128 - 16 * q, 1) for q in range(1, nt - 1)]
        tiles.append(tops[:, 128:256])
        spread = jnp.where((ec // RATIO) == er, 1.0, 0.0)
        u = jnp.dot(jnp.concatenate(tiles, axis=0), spread,
                    preferred_element_type=F32, precision=lax.Precision.HIGHEST)
        for q in range(nt):
            r = u[8 * q:8 * q + 8, :]
            e = [jnp.broadcast_to(r[i:i + 1, :], (24, 128)) for i in range(4)]
            full = jnp.where(row24 < 8, e[0], jnp.where(row24 < 16, e[1], jnp.where(row24 < 20, e[2], e[3])))
            at = slice(128 * q, 128 * q + 128)
            Up[:, at] = full
        H[...] = H[...] + UPLIFT_GAIN * W[...] * Up[...]

    def average(slot):
        p = W[0:16, 0:own] * H[0:16, 0:own]
        parts = [p[:, 128 * q:128 * q + 128] for q in range(nt - 1)]
        gather = jnp.where((er // RATIO) == ec, 1.0, 0.0)
        g = jnp.dot(jnp.concatenate(parts, axis=0), gather,
                    preferred_element_type=F32, precision=lax.Precision.HIGHEST)
        a0 = jnp.zeros((1, 128), F32)
        a1 = jnp.zeros((1, 128), F32)
        for q in range(nt - 1):
            s0 = jnp.sum(g[16 * q:16 * q + 8, :], axis=0, keepdims=True)
            s1 = jnp.sum(g[16 * q + 8:16 * q + 16, :], axis=0, keepdims=True)
            two = jnp.concatenate([s0, s1, jnp.zeros((6, 128), F32)], axis=0)
            if q:
                two = pltpu.roll(two, 16 * q, 1)
            a0 = a0 + two[0:1, :]
            a1 = a1 + two[1:2, :]
        scale = -LOAD_GAIN / (RATIO * RATIO)
        ls[slot, 0:1, :] = a0 * scale
        ls[slot, 1:2, :] = a1 * scale

    def apply_load(slot):
        lm(slot).got()
        S[2, 0, 0:1, :] = ls[slot, 1:2, :]
        S[2, 1, 0:1, :] = lr[slot, 0:1, :]

    def motion_part(z):
        zs = slice(z, z + size)
        for x in range(2):
            sb = SOLID_STEP * Bu[x, zs]
            xx, yy, zz, xz, xy, yz = (S[c, x, zs] for c in range(6))
            xx_a = S[0, 1, zs] if x == 0 else ha_xx[zs]
            xz_b = hb_s[0, zs] if x == 0 else S[3, 0, zs]
            xy_b = hb_s[1, zs] if x == 0 else S[4, 0, zs]
            V[2, x, zs] = V[2, x, zs] + sb * (
                (xx_a - xx) + (xy - ym(xy, hd_s[0, x, zs])) + (xz - zm(S, 3, x, z)))
            V[0, x, zs] = V[0, x, zs] + sb * (
                (xy - xy_b) + (yp(yy, hu_yy[x, zs]) - yy) + (yz - zm(S, 5, x, z)))
            V[1, x, zs] = V[1, x, zs] + sb * (
                (xz - xz_b) + (yz - ym(yz, hd_s[1, x, zs])) + (zp(S, 2, x, z) - zz))

    def stress_part(z):
        zs = slice(z, z + size)
        for x in range(2):
            vy, vz, vx = V[0, x, zs], V[1, x, zs], V[2, x, zs]
            vx_b = hb_vx[zs] if x == 0 else V[2, 0, zs]
            vy_a = V[0, 1, zs] if x == 0 else ha_v[0, zs]
            vz_a = V[1, 1, zs] if x == 0 else ha_v[1, zs]
            ex = vx - vx_b
            ey = vy - ym(vy, hd_vy[x, zs])
            ez = vz - zm(V, 1, x, z)
            l, g = SOLID_STEP * L1[x, zs], SOLID_STEP * L2[x, zs]
            tr = l * (ex + ey + ez)
            g2 = 2.0 * g
            S[0, x, zs] = S[0, x, zs] + (tr + g2 * ex)
            S[1, x, zs] = S[1, x, zs] + (tr + g2 * ey)
            S[2, x, zs] = S[2, x, zs] + (tr + g2 * ez)
            S[3, x, zs] = S[3, x, zs] + g * ((zp(V, 2, x, z) - vx) + (vz_a - vz))
            S[4, x, zs] = S[4, x, zs] + g * ((yp(vx, hu_v[1, x, zs]) - vx) + (vy_a - vy))
            S[5, x, zs] = S[5, x, zs] + g * ((zp(V, 0, x, z) - vy) + (yp(vz, hu_v[0, x, zs]) - vz))

    def step(k, carry):
        slot = lax.rem(k, 2)
        nslot = lax.rem(k + 1, 2)

        xms = xm(slot)
        cms = cm(slot)
        for m in xms:
            m.got()
        use_x(slot)

        @pl.when(k == 0)
        def _():
            for m in xsm:
                m.got()
            bed_x()
            start_all(csm)

        fill_c(slot)
        start_all(cms)

        for p in range(PARTS):
            for m in am[p]:
                m.got()
            if p == 0:
                @pl.when(k > 0)
                def _():
                    apply_load(nslot)

            motion_part(p * size)
            start_all(bm[p])

        for m in cms:
            m.got()
        use_c(slot)

        @pl.when(k == 0)
        def _():
            for m in csm:
                m.got()
            ocean_setup()
            mask_flow()

        lift()
        lax.fori_loop(0, NSUB, substep, 0)
        average(slot)
        lm(slot).start()

        @pl.when(k < STEPS - 1)
        def _():
            fill_x(nslot)
            start_all(xm(nslot))

        for p in range(PARTS):
            for m in bm[p]:
                m.got()
            for m in am[p]:
                m.sent()
            stress_part(p * size)

            @pl.when(k < STEPS - 1)
            def _():
                start_all(am[p])

        for ms in bm:
            for m in ms:
                m.sent()
        for m in xms + cms:
            m.sent()
        lm(slot).sent()
        return carry

    lax.fori_loop(0, STEPS, step, 0)
    for m in xsm + csm:
        m.sent()
    apply_load((STEPS - 1) % 2)
    outs = [
        pltpu.make_async_copy(a, b, in_sem.at[i])
        for i, (a, b) in enumerate([
            (V.at[pl.ds(0, 2)], o_motion.at[pl.ds(1, 2)]), (V.at[2], o_motion.at[0]),
            (S.at[pl.ds(0, 3)], o_stress.at[pl.ds(0, 3)]), (S.at[4], o_stress.at[3]),
            (S.at[3], o_stress.at[4]), (S.at[5], o_stress.at[5]),
            (H.at[pl.ds(0, 16), pl.ds(0, own)], o_surf),
            (M.at[pl.ds(0, 16), pl.ds(0, own)], o_mom.at[0]),
            (N.at[pl.ds(0, 16), pl.ds(0, own)], o_mom.at[1]),
        ])
    ]
    for c in outs:
        c.start()
    for c in outs:
        c.wait()


def body(nx, ny, motion, stress, buoyancy, lame_first, lame_shear, surface, momentum, bathymetry, wet_mask):
    plane = motion.shape[2:]
    two = motion.shape[1:]
    ext = (24, surface.shape[1] + 128)

    def v(*shape):
        return pltpu.VMEM(shape, F32)

    scratch = [v(*stress.shape), v(*motion.shape)] + [v(*two)] * 3
    scratch += [v(*ext)] * 3 + [pltpu.VMEM(wet_mask.shape, jnp.int32)] + [v(*ext)] * 11
    scratch += [v(2, *plane), v(*plane), v(2, *two), v(*two)]
    scratch += [v(*plane), v(2, *plane), v(*two), v(2, *two)]
    scratch += [v(2, 80, 128)] * 4 + [v(72, 128)] * 4
    wide = surface.shape[1]
    scratch += [v(2, 8, wide + wide // 2 + 128)] * 4 + [v(8, wide + 128)] * 4
    scratch += [v(2, 8, 128), v(2, 8, 128), v(8, 256)]
    dma = pltpu.SemaphoreType.DMA
    scratch += [dma((14,)), dma((8 * PARTS + 4,)), dma((8 * PARTS + 4,)), dma((2, 2)), dma((2, 2)), dma((2, 2)), dma((2, 2)), dma((2,)), dma((2,))]
    return pl.pallas_call(
        functools.partial(kernel, nx, ny),
        out_shape=[
            jax.ShapeDtypeStruct(a.shape, F32) for a in (motion, stress, surface, momentum)
        ],
        in_specs=[pl.BlockSpec(memory_space=pltpu.HBM)] * 9,
        out_specs=[pl.BlockSpec(memory_space=pltpu.HBM)] * 4,
        scratch_shapes=scratch,
        compiler_params=pltpu.CompilerParams(
            collective_id=0, has_side_effects=True, vmem_limit_bytes=60 * 1024 * 1024
        ),
        name="coupled",
    )(motion, stress, buoyancy, lame_first, lame_shear, surface, momentum, bathymetry, wet_mask)


def solution(mesh):
    return jax.shard_map(
        functools.partial(body, mesh.shape["gx"], mesh.shape["gy"]),
        mesh=mesh,
        in_specs=(
            P(None, "gx", None, "gy"),
            P(None, "gx", None, "gy"),
            P("gx", None, "gy"),
            P("gx", None, "gy"),
            P("gx", None, "gy"),
            P("gx", "gy"),
            P(None, "gx", "gy"),
            P("gx", "gy"),
            P("gx", "gy"),
        ),
        out_specs=(
            P(None, "gx", None, "gy"),
            P(None, "gx", None, "gy"),
            P("gx", "gy"),
            P(None, "gx", "gy"),
        ),
        check_vma=False,
    )
```

time: 69.9 us -> 54.2 us (0.78)
  Pallas kernels: 57.9 us -> 49 us
  local copies, waits for them, and re-layouts: 10.9 us -> 4.2 us
    pallas_call x1, Pallas kernels: 57.9 us -> 49 us  [body(): pl.pallas_call(functools.partial(kernel, nx, ny), out_shape=[jax.ShapeDty...]
    unnamed x22 -> x10, local copies, waits for them, and re-layouts: 10.9 us -> 4.2 us
where the time goes in v1:
time: 54.2 us; the launch traced here: 53.9 us
  Pallas kernels  49 us (90%)
  local copies, waits for them, and re-layouts  4.2 us (8%)
  between operations  0.65 us (1%)
    pallas_call x1, Pallas kernels, body(): pl.pallas_call(functools.partial(kernel, nx, ny), out_shape=[jax.ShapeDty...  49 us
    unnamed x10, local copies, waits for them, and re-layouts  4.2 us

profile of v1, /device:TPU:0, one launch (start us, length us, event | category | flops | bytes accessed | tf_op | source)
XLA Modules:
  0.0 53.9 jit_solution(16635774404597610023)
XLA Ops:
  0.6 49.0 %coupled.1 = (f32[3,2,96,128]{3,2,1,0:T(8,128)}, f32[6,2,96,128]{3,2,1,0:T(8,128)}, f32[16,1024]{1,0:T(8,128)}, f32[2,16,1024]{2,1,0:T(8,128)}) custom-call(f32[3,2,96,128]{3,2,1,0:T(8,128)} %motion.1, f32[6,2,96,128]{3,2,1,0:T(8,128)} %stress.1, f32[2,96,128]{2,1,0:T(8,128)} %buoy.1, f32[2,96,128]{2,1,0:T(8,128)} %lame1.1, f32[2,96,128]{2,1,0:T(8,128)} %lame2.1, ...), custom_call_target="tpu_custom_call" | custom-call | tf_op jit(solution)/shard_map/coupled/pallas_call | solution.py:484
  49.7 0.0 copy-start
  49.7 1.8 %copy.17 = f32[3,2,96,128]{3,2,1,0:T(8,128)} copy(f32[3,2,96,128]{3,2,1,0:T(8,128)} %get-tuple-element.8) | data formatting | bytes 589824
  51.5 0.0 copy-done
  51.5 0.0 copy-start.2
  51.5 0.8 %copy.18 = f32[6,2,96,128]{3,2,1,0:T(8,128)} copy(f32[6,2,96,128]{3,2,1,0:T(8,128)S(1)} %copy-done) | data formatting | bytes 1179648
  52.3 0.0 copy-done.2
  52.3 0.0 copy-start.1
  52.3 0.6 %copy.19 = f32[16,1024]{1,0:T(8,128)} copy(f32[16,1024]{1,0:T(8,128)S(1)} %copy-done.2) | data formatting | bytes 131072
  53.0 0.3 copy-done.1
  53.3 0.7 %copy.20 = f32[2,16,1024]{2,1,0:T(8,128)} copy(f32[2,16,1024]{2,1,0:T(8,128)S(1)} %copy-done.1) | data formatting | bytes 262144
Async XLA Ops:
  49.7 1.8 %copy-start = (f32[6,2,96,128]{3,2,1,0:T(8,128)S(1)}, f32[6,2,96,128]{3,2,1,0:T(8,128)}, u32[]{:S(2)}) copy-start(f32[6,2,96,128]{3,2,1,0:T(8,128)} %get-tuple-element.9) | copy-start | bytes 1769476
  51.5 0.9 %copy-start.2 = (f32[16,1024]{1,0:T(8,128)S(1)}, f32[16,1024]{1,0:T(8,128)}, u32[]{:S(2)}) copy-start(f32[16,1024]{1,0:T(8,128)} %get-tuple-element.10) | copy-start | bytes 196612
  52.3 0.9 %copy-start.1 = (f32[2,16,1024]{2,1,0:T(8,128)S(1)}, f32[2,16,1024]{2,1,0:T(8,128)}, u32[]{:S(2)}) copy-start(f32[2,16,1024]{2,1,0:T(8,128)} %get-tuple-element.11) | copy-start | bytes 393220

commit v2 on v1

--- a/solution.py
+++ b/solution.py
@@ -24,8 +24,8 @@
 def kernel(
     nx, ny,
     motion, stress, buoy, lame1, lame2, surf, mom, bath, wetm,
-    o_motion, o_stress, o_surf, o_mom,
-    S, V, Bu, L1, L2, H, M, N, Wi, W, D, wt, Dx, Dy, Ax, Bx, Ay, By, Fx, Up,
+    V, S, H, M, N,
+    Bu, L1, L2, Wi, W, D, wt, Dx, Dy, Ax, Bx, Ay, By, Fx, Up,
     hb_s, ha_xx, hd_s, hu_yy,
     hb_vx, ha_v, hd_vy, hu_v,
     cu, cd, hd_c, hu_c, csu, csd, hd_cs, hu_cs,
@@ -296,13 +296,21 @@
     ec = lax.broadcasted_iota(jnp.int32, (128, 128), 1)
     row24 = lax.broadcasted_iota(jnp.int32, (24, 128), 0)
 
+    def spread_dot(a, ones):
+        p0 = a.astype(jnp.bfloat16)
+        r = a - p0.astype(F32)
+        p1 = r.astype(jnp.bfloat16)
+        p2 = (r - p1.astype(F32)).astype(jnp.bfloat16)
+        e = ones.astype(jnp.bfloat16)
+        return jnp.dot(jnp.concatenate([p0, p1, p2], axis=1),
+                       jnp.concatenate([e, e, e], axis=0), preferred_element_type=F32)
+
     def lift():
         t = tops[:, 0:128]
         tiles = [t] + [pltpu.roll(t, 128 - 16 * q, 1) for q in range(1, nt - 1)]
         tiles.append(tops[:, 128:256])
         spread = jnp.where((ec // RATIO) == er, 1.0, 0.0)
-        u = jnp.dot(jnp.concatenate(tiles, axis=0), spread,
-                    preferred_element_type=F32, precision=lax.Precision.HIGHEST)
+        u = spread_dot(jnp.concatenate(tiles, axis=0), spread)
         for q in range(nt):
             r = u[8 * q:8 * q + 8, :]
             e = [jnp.broadcast_to(r[i:i + 1, :], (24, 128)) for i in range(4)]
@@ -315,21 +323,15 @@
         p = W[0:16, 0:own] * H[0:16, 0:own]
         parts = [p[:, 128 * q:128 * q + 128] for q in range(nt - 1)]
         gather = jnp.where((er // RATIO) == ec, 1.0, 0.0)
-        g = jnp.dot(jnp.concatenate(parts, axis=0), gather,
-                    preferred_element_type=F32, precision=lax.Precision.HIGHEST)
-        a0 = jnp.zeros((1, 128), F32)
-        a1 = jnp.zeros((1, 128), F32)
-        for q in range(nt - 1):
-            s0 = jnp.sum(g[16 * q:16 * q + 8, :], axis=0, keepdims=True)
-            s1 = jnp.sum(g[16 * q + 8:16 * q + 16, :], axis=0, keepdims=True)
-            two = jnp.concatenate([s0, s1, jnp.zeros((6, 128), F32)], axis=0)
-            if q:
-                two = pltpu.roll(two, 16 * q, 1)
-            a0 = a0 + two[0:1, :]
-            a1 = a1 + two[1:2, :]
+        g = spread_dot(jnp.concatenate(parts, axis=0), gather)
+        a0, a1 = g[0:8, :], g[8:16, :]
+        for q in range(1, nt - 1):
+            a0 = a0 + pltpu.roll(g[16 * q:16 * q + 8, :], 16 * q, 1)
+            a1 = a1 + pltpu.roll(g[16 * q + 8:16 * q + 16, :], 16 * q, 1)
         scale = -LOAD_GAIN / (RATIO * RATIO)
-        ls[slot, 0:1, :] = a0 * scale
-        ls[slot, 1:2, :] = a1 * scale
+        ls[slot, 0:1, :] = jnp.sum(a0, axis=0, keepdims=True) * scale
+        ls[slot, 1:2, :] = jnp.sum(a1, axis=0, keepdims=True) * scale
+        lm(slot).start()
 
     def apply_load(slot):
         lm(slot).got()
@@ -390,6 +392,18 @@
 
         fill_c(slot)
         start_all(cms)
+        for m in cms:
+            m.got()
+        use_c(slot)
+
+        @pl.when(k == 0)
+        def _():
+            for m in csm:
+                m.got()
+            ocean_setup()
+            mask_flow()
+
+        lift()
 
         for p in range(PARTS):
             for m in am[p]:
@@ -401,22 +415,10 @@
 
             motion_part(p * size)
             start_all(bm[p])
-
-        for m in cms:
-            m.got()
-        use_c(slot)
-
-        @pl.when(k == 0)
-        def _():
-            for m in csm:
-                m.got()
-            ocean_setup()
-            mask_flow()
-
-        lift()
-        lax.fori_loop(0, NSUB, substep, 0)
-        average(slot)
-        lm(slot).start()
+            lax.fori_loop(NSUB * p // PARTS, NSUB * (p + 1) // PARTS, substep, 0)
+
+        last = k == STEPS - 1
+        pl.when(last)(lambda: average(slot))
 
         @pl.when(k < STEPS - 1)
         def _():
@@ -434,6 +436,7 @@
             def _():
                 start_all(am[p])
 
+        pl.when(jnp.logical_not(last))(lambda: average(slot))
         for ms in bm:
             for m in ms:
                 m.sent()
@@ -446,15 +449,18 @@
     for m in xsm + csm:
         m.sent()
     apply_load((STEPS - 1) % 2)
+
+
+def write_out(V, S, H, M, N, o_motion, o_stress, o_surf, o_mom, sem):
+    rows, own = o_surf.shape
+    at = (pl.ds(0, rows), pl.ds(0, own))
     outs = [
-        pltpu.make_async_copy(a, b, in_sem.at[i])
+        pltpu.make_async_copy(a, b, sem.at[i])
         for i, (a, b) in enumerate([
+            (S.at[pl.ds(0, 3)], o_stress.at[pl.ds(0, 3)]),
             (V.at[pl.ds(0, 2)], o_motion.at[pl.ds(1, 2)]), (V.at[2], o_motion.at[0]),
-            (S.at[pl.ds(0, 3)], o_stress.at[pl.ds(0, 3)]), (S.at[4], o_stress.at[3]),
-            (S.at[3], o_stress.at[4]), (S.at[5], o_stress.at[5]),
-            (H.at[pl.ds(0, 16), pl.ds(0, own)], o_surf),
-            (M.at[pl.ds(0, 16), pl.ds(0, own)], o_mom.at[0]),
-            (N.at[pl.ds(0, 16), pl.ds(0, own)], o_mom.at[1]),
+            (S.at[4], o_stress.at[3]), (S.at[3], o_stress.at[4]), (S.at[5], o_stress.at[5]),
+            (H.at[at], o_surf), (M.at[at], o_mom.at[0]), (N.at[at], o_mom.at[1]),
         ])
     ]
     for c in outs:
@@ -471,8 +477,7 @@
     def v(*shape):
         return pltpu.VMEM(shape, F32)
 
-    scratch = [v(*stress.shape), v(*motion.shape)] + [v(*two)] * 3
-    scratch += [v(*ext)] * 3 + [pltpu.VMEM(wet_mask.shape, jnp.int32)] + [v(*ext)] * 11
+    scratch = [v(*two)] * 3 + [pltpu.VMEM(wet_mask.shape, jnp.int32)] + [v(*ext)] * 11
     scratch += [v(2, *plane), v(*plane), v(2, *two), v(*two)]
     scratch += [v(*plane), v(2, *plane), v(*two), v(2, *two)]
     scratch += [v(2, 80, 128)] * 4 + [v(72, 128)] * 4
@@ -481,19 +486,29 @@
     scratch += [v(2, 8, 128), v(2, 8, 128), v(8, 256)]
     dma = pltpu.SemaphoreType.DMA
     scratch += [dma((14,)), dma((8 * PARTS + 4,)), dma((8 * PARTS + 4,)), dma((2, 2)), dma((2, 2)), dma((2, 2)), dma((2, 2)), dma((2,)), dma((2,))]
+    state = [motion.shape, stress.shape, ext, ext, ext]
+    hbm = pl.BlockSpec(memory_space=pltpu.HBM)
+    held = pl.pallas_call(
+        functools.partial(kernel, nx, ny),
+        out_shape=[pltpu.VMEM(shape, F32) for shape in state],
+        in_specs=[hbm] * 9,
+        out_specs=[pl.BlockSpec(memory_space=pltpu.VMEM)] * 5,
+        scratch_shapes=scratch,
+        compiler_params=pltpu.CompilerParams(
+            collective_id=0, has_side_effects=True, vmem_limit_bytes=56 * 1024 * 1024
+        ),
+        name="coupled",
+    )(motion, stress, buoyancy, lame_first, lame_shear, surface, momentum, bathymetry, wet_mask)
     return pl.pallas_call(
-        functools.partial(kernel, nx, ny),
+        write_out,
         out_shape=[
             jax.ShapeDtypeStruct(a.shape, F32) for a in (motion, stress, surface, momentum)
         ],
-        in_specs=[pl.BlockSpec(memory_space=pltpu.HBM)] * 9,
-        out_specs=[pl.BlockSpec(memory_space=pltpu.HBM)] * 4,
-        scratch_shapes=scratch,
-        compiler_params=pltpu.CompilerParams(
-            collective_id=0, has_side_effects=True, vmem_limit_bytes=60 * 1024 * 1024
-        ),
-        name="coupled",
-    )(motion, stress, buoyancy, lame_first, lame_shear, surface, momentum, bathymetry, wet_mask)
+        in_specs=[pl.BlockSpec(memory_space=pl.ANY)] * 5,
+        out_specs=[pl.BlockSpec(memory_space=pl.ANY)] * 4,
+        scratch_shapes=[dma((9,))],
+        name="write_out",
+    )(*held)
 
 
 def solution(mesh):

time: 54.2 us -> 90 us (1.66)
  Pallas kernels: 49 us -> 85.8 us
    pallas_call x1 -> x2, Pallas kernels: 49 us -> 85.8 us  [the longest x1 51.8 us: body(): pl.pallas_call(functools.partial(kernel, nx, ny), out_shape=[pltpu.VMEM(s...]
where the time goes in v2:
time: 90 us; the launch traced here: 89.9 us
  Pallas kernels  85.8 us (95%)
  local copies, waits for them, and re-layouts  3.47 us (4%)
    pallas_call x1, Pallas kernels, body(): pl.pallas_call(functools.partial(kernel, nx, ny), out_shape=[pltpu.VMEM(s...  51.8 us
    pallas_call x1, Pallas kernels, body(): pl.pallas_call(write_out, out_shape=[jax.ShapeDtypeStruct(a.shape, F32) f...  33.9 us
    unnamed x10, local copies, waits for them, and re-layouts  3.47 us

profile of v2, /device:TPU:0, one launch (start us, length us, event | category | flops | bytes accessed | tf_op | source)
XLA Modules:
  0.0 89.9 jit_solution(9188932173994359426)
XLA Ops:
  0.6 51.8 %coupled.1 = (f32[3,2,96,128]{3,2,1,0:T(8,128)S(1)}, f32[6,2,96,128]{3,2,1,0:T(8,128)S(1)}, f32[24,1152]{1,0:T(8,128)S(1)}, f32[24,1152]{1,0:T(8,128)S(1)}, f32[24,1152]{1,0:T(8,128)S(1)}) custom-call(f32[3,2,96,128]{3,2,1,0:T(8,128)} %motion.1, f32[6,2,96,128]{3,2,1,0:T(8,128)} %stress.1, f32[2,96,128]{2,1,0:T(8,128)} %buoy.1, f32[2,96,128]{2,1,0:T(8,128)} %lame1.1, ...), custom_call_target="tpu_custom_call" | custom-call | tf_op jit(solution)/shard_map/coupled/pallas_call | solution.py:491
  52.5 0.0 copy-start
  52.5 0.8 copy-done
  53.3 0.0 copy-start.1
  53.3 0.7 copy-done.1
  54.0 0.0 copy-start.2
  54.0 0.7 copy-done.2
  54.7 0.0 copy-start.3
  54.7 0.6 copy-done.3
  55.3 0.0 copy-start.4
  55.3 0.7 copy-done.4
  56.0 33.9 %write_out.1 = (f32[3,2,96,128]{3,2,1,0:T(8,128)}, f32[6,2,96,128]{3,2,1,0:T(8,128)}, f32[16,1024]{1,0:T(8,128)}, f32[2,16,1024]{2,1,0:T(8,128)}) custom-call(f32[3,2,96,128]{3,2,1,0:T(8,128)} %copy-done.1, f32[6,2,96,128]{3,2,1,0:T(8,128)} %copy-done, f32[24,1152]{1,0:T(8,128)} %copy-done.2, f32[24,1152]{1,0:T(8,128)} %copy-done.3, f32[24,1152]{1,0:T(8,128)} %copy-done.4), custom_call_target="tpu_custom_call" | custom-call | tf_op jit(solution)/shard_map/write_out/pallas_call | solution.py:502
Async XLA Ops:
  52.5 0.8 copy-start
  53.3 0.7 copy-start.1
  54.0 0.7 copy-start.2
  54.7 0.6 copy-start.3
  55.3 0.7 copy-start.4

commit v3 on v2

--- a/solution.py
+++ b/solution.py
@@ -25,7 +25,7 @@
     nx, ny,
     motion, stress, buoy, lame1, lame2, surf, mom, bath, wetm,
     V, S, H, M, N,
-    Bu, L1, L2, Wi, W, D, wt, Dx, Dy, Ax, Bx, Ay, By, Fx, Up,
+    Bu, L1, L2, Wi, W, D, wt, Dx, Dy, Ax, Bx, Ay, By, Fx,
     hb_s, ha_xx, hd_s, hu_yy,
     hb_vx, ha_v, hd_vy, hu_v,
     cu, cd, hd_c, hu_c, csu, csd, hd_cs, hu_cs,
@@ -280,16 +280,45 @@
         M[...] = mm
         N[...] = nn
 
+    first24, last24 = lane24 == 0, lane24 == 127
+
+    def tile(r, q):
+        q = q % nt
+        return r[:, 128 * q:128 * q + 128]
+
+    def from_left(a, left):
+        return pltpu.roll(jnp.where(last24, left, a), 1, 1)
+
+    def from_right(a, right):
+        return pltpu.roll(jnp.where(first24, right, a), 127, 1)
+
     def substep(_, carry):
-        m, n = M[...], N[...]
-        mw, ns = rm(m), cmn(n)
-        h = H[...] - wt[...] * ((m - mw) + (n - ns))
-        H[...] = h
-        he, hn = rp(h), cpl(h)
-        M[...] = Ax[...] * m + Bx[...] * (
-            ((rp(m) + mw) + (cpl(m) + cmn(m))) - (Dx[...] + h + he) * (he - h))
-        N[...] = Ay[...] * n + By[...] * (
-            ((rp(n) + rm(n)) + (cpl(n) + ns)) - (Dy[...] + h + hn) * (hn - h))
+        m0, n0 = tile(M, 0), tile(N, 0)
+        ml, nl = tile(M, nt - 1), tile(N, nt - 1)
+        m, n = m0, n0
+
+        def height(q, m, n, nl):
+            mw, ns = rm(m), from_left(n, nl)
+            return tile(H, q) - tile(wt, q) * ((m - mw) + (n - ns)), mw, ns
+
+        h0, mw, ns = height(0, m, n, nl)
+        h = h0
+        for q in range(nt):
+            at = slice(128 * q, 128 * q + 128)
+            H[:, at] = h
+            if q < nt - 1:
+                mr, nr = tile(M, q + 1), tile(N, q + 1)
+                hr, mwr, nsr = height(q + 1, mr, nr, n)
+            else:
+                mr, nr, hr, mwr, nsr = m0, n0, h0, None, None
+            he, hn = rp(h), from_right(h, hr)
+            M[:, at] = tile(Ax, q) * m + tile(Bx, q) * (
+                ((rp(m) + mw) + (from_right(m, mr) + from_left(m, ml)))
+                - (tile(Dx, q) + h + he) * (he - h))
+            N[:, at] = tile(Ay, q) * n + tile(By, q) * (
+                ((rp(n) + rm(n)) + (from_right(n, nr) + ns))
+                - (tile(Dy, q) + h + hn) * (hn - h))
+            ml, m, n, h, mw, ns = m, mr, nr, hr, mwr, nsr
         return carry
 
     er = lax.broadcasted_iota(jnp.int32, (128, 128), 0)
@@ -316,8 +345,7 @@
             e = [jnp.broadcast_to(r[i:i + 1, :], (24, 128)) for i in range(4)]
             full = jnp.where(row24 < 8, e[0], jnp.where(row24 < 16, e[1], jnp.where(row24 < 20, e[2], e[3])))
             at = slice(128 * q, 128 * q + 128)
-            Up[:, at] = full
-        H[...] = H[...] + UPLIFT_GAIN * W[...] * Up[...]
+            H[:, at] = H[:, at] + UPLIFT_GAIN * W[:, at] * full
 
     def average(slot):
         p = W[0:16, 0:own] * H[0:16, 0:own]
@@ -392,18 +420,6 @@
 
         fill_c(slot)
         start_all(cms)
-        for m in cms:
-            m.got()
-        use_c(slot)
-
-        @pl.when(k == 0)
-        def _():
-            for m in csm:
-                m.got()
-            ocean_setup()
-            mask_flow()
-
-        lift()
 
         for p in range(PARTS):
             for m in am[p]:
@@ -415,8 +431,20 @@
 
             motion_part(p * size)
             start_all(bm[p])
-            lax.fori_loop(NSUB * p // PARTS, NSUB * (p + 1) // PARTS, substep, 0)
-
+
+        for m in cms:
+            m.got()
+        use_c(slot)
+
+        @pl.when(k == 0)
+        def _():
+            for m in csm:
+                m.got()
+            ocean_setup()
+            mask_flow()
+
+        lift()
+        lax.fori_loop(0, NSUB, substep, 0)
         last = k == STEPS - 1
         pl.when(last)(lambda: average(slot))
 
@@ -477,7 +505,7 @@
     def v(*shape):
         return pltpu.VMEM(shape, F32)
 
-    scratch = [v(*two)] * 3 + [pltpu.VMEM(wet_mask.shape, jnp.int32)] + [v(*ext)] * 11
+    scratch = [v(*two)] * 3 + [pltpu.VMEM(wet_mask.shape, jnp.int32)] + [v(*ext)] * 10
     scratch += [v(2, *plane), v(*plane), v(2, *two), v(*two)]
     scratch += [v(*plane), v(2, *plane), v(*two), v(2, *two)]
     scratch += [v(2, 80, 128)] * 4 + [v(72, 128)] * 4
@@ -507,6 +535,7 @@
         in_specs=[pl.BlockSpec(memory_space=pl.ANY)] * 5,
         out_specs=[pl.BlockSpec(memory_space=pl.ANY)] * 4,
         scratch_shapes=[dma((9,))],
+        compiler_params=pltpu.CompilerParams(vmem_limit_bytes=1024 * 1024),
         name="write_out",
     )(*held)
 

time: 90 us -> 52.4 us (0.58)
  the two profiles are of different devices: /device:TPU:0 before, /device:TPU:6 now
where the time goes in v3:
time: 52.4 us; the launch traced here: 52.3 us
  Pallas kernels  51.6 us (98%)
  between operations  0.64 us (1%)
    pallas_call x1, Pallas kernels, body(): pl.pallas_call(functools.partial(kernel, nx, ny), out_shape=[pltpu.VMEM(s...  50.6 us

profile of v3, /device:TPU:6, one launch (start us, length us, event | category | flops | bytes accessed | tf_op | source)
XLA Modules:
  0.0 52.3 jit_solution(10360407813152930101)
XLA Ops:
  0.6 50.6 %coupled.1 = (f32[3,2,96,128]{3,2,1,0:T(8,128)S(1)}, f32[6,2,96,128]{3,2,1,0:T(8,128)S(1)}, f32[24,1152]{1,0:T(8,128)S(1)}, f32[24,1152]{1,0:T(8,128)S(1)}, f32[24,1152]{1,0:T(8,128)S(1)}) custom-call(f32[3,2,96,128]{3,2,1,0:T(8,128)} %motion.1, f32[6,2,96,128]{3,2,1,0:T(8,128)} %stress.1, f32[2,96,128]{2,1,0:T(8,128)} %buoy.1, f32[2,96,128]{2,1,0:T(8,128)} %lame1.1, ...), custom_call_target="tpu_custom_call" | custom-call | tf_op jit(solution)/shard_map/coupled/pallas_call | solution.py:519
  51.2 1.0 %write_out.1 = (f32[3,2,96,128]{3,2,1,0:T(8,128)}, f32[6,2,96,128]{3,2,1,0:T(8,128)}, f32[16,1024]{1,0:T(8,128)}, f32[2,16,1024]{2,1,0:T(8,128)}) custom-call(f32[3,2,96,128]{3,2,1,0:T(8,128)S(1)} %get-tuple-element.9.V, f32[6,2,96,128]{3,2,1,0:T(8,128)S(1)} %get-tuple-element.10.S, f32[24,1152]{1,0:T(8,128)S(1)} %get-tuple-element.11.H, ...), custom_call_target="tpu_custom_call" | custom-call | tf_op jit(solution)/shard_map/write_out/pallas_call | solution.py:530

commit v4 on v3

--- a/solution.py
+++ b/solution.py
@@ -10,7 +10,7 @@
 RATIO = 8
 STEPS = 4
 NSUB = 4
-PARTS = 2
+PARTS = 3
 SOLID_STEP = 0.2
 WAVE_STEP = 0.1
 VISCOSITY = 0.05
@@ -54,14 +54,14 @@
     loads = [
         pltpu.make_async_copy(a, b, in_sem.at[i])
         for i, (a, b) in enumerate([
+            (stress.at[pl.ds(0, 3)], S.at[pl.ds(0, 3)]), (stress.at[3], S.at[4]),
+            (stress.at[4], S.at[3]), (stress.at[5], S.at[5]),
             (wetm, Wi),
             (bath, D.at[pl.ds(0, 16), pl.ds(0, own)]),
             (surf, H.at[pl.ds(0, 16), pl.ds(0, own)]),
             (mom.at[0], M.at[pl.ds(0, 16), pl.ds(0, own)]),
             (mom.at[1], N.at[pl.ds(0, 16), pl.ds(0, own)]),
             (motion.at[pl.ds(1, 2)], V.at[pl.ds(0, 2)]), (motion.at[0], V.at[2]),
-            (stress.at[pl.ds(0, 3)], S.at[pl.ds(0, 3)]), (stress.at[3], S.at[4]),
-            (stress.at[4], S.at[3]), (stress.at[5], S.at[5]),
             (buoy, Bu), (lame1, L1), (lame2, L2),
         ])
     ]
@@ -223,11 +223,11 @@
         for m in ms:
             m.start()
 
-    for c in loads[7:11]:
+    for c in loads[:4]:
         c.wait()
     for p in range(PARTS):
         start_all(am[p])
-    for c in loads[:7]:
+    for c in loads[4:11]:
         c.wait()
     W[0:16, 0:own] = Wi[...].astype(F32)
     for buf, rows in ((xsf, slice(12, 16)), (xsb, slice(0, 4))):

time: 52.4 us -> 52.9 us (level)
  no operation moved by 1% of the time
where the time goes in v4:
time: 52.9 us; the launch traced here: 52.7 us
  Pallas kernels  52.1 us (98%)
  between operations  0.64 us (1%)
    pallas_call x1, Pallas kernels, body(): pl.pallas_call(functools.partial(kernel, nx, ny), out_shape=[pltpu.VMEM(s...  51 us

profile of v4, /device:TPU:6, one launch (start us, length us, event | category | flops | bytes accessed | tf_op | source)
XLA Modules:
  0.0 52.7 jit_solution(18048803732423105774)
XLA Ops:
  0.6 51.0 %coupled.1 = (f32[3,2,96,128]{3,2,1,0:T(8,128)S(1)}, f32[6,2,96,128]{3,2,1,0:T(8,128)S(1)}, f32[24,1152]{1,0:T(8,128)S(1)}, f32[24,1152]{1,0:T(8,128)S(1)}, f32[24,1152]{1,0:T(8,128)S(1)}) custom-call(f32[3,2,96,128]{3,2,1,0:T(8,128)} %motion.1, f32[6,2,96,128]{3,2,1,0:T(8,128)} %stress.1, f32[2,96,128]{2,1,0:T(8,128)} %buoy.1, f32[2,96,128]{2,1,0:T(8,128)} %lame1.1, ...), custom_call_target="tpu_custom_call" | custom-call | tf_op jit(solution)/shard_map/coupled/pallas_call | solution.py:519
  51.7 1.0 %write_out.1 = (f32[3,2,96,128]{3,2,1,0:T(8,128)}, f32[6,2,96,128]{3,2,1,0:T(8,128)}, f32[16,1024]{1,0:T(8,128)}, f32[2,16,1024]{2,1,0:T(8,128)}) custom-call(f32[3,2,96,128]{3,2,1,0:T(8,128)S(1)} %get-tuple-element.9.V, f32[6,2,96,128]{3,2,1,0:T(8,128)S(1)} %get-tuple-element.10.S, f32[24,1152]{1,0:T(8,128)S(1)} %get-tuple-element.11.H, ...), custom_call_target="tpu_custom_call" | custom-call | tf_op jit(solution)/shard_map/write_out/pallas_call | solution.py:530

commit v5 on v4

--- a/solution.py
+++ b/solution.py
@@ -10,7 +10,7 @@
 RATIO = 8
 STEPS = 4
 NSUB = 4
-PARTS = 3
+PARTS = 2
 SOLID_STEP = 0.2
 WAVE_STEP = 0.1
 VISCOSITY = 0.05
@@ -236,8 +236,6 @@
     for q in range(own // 128):
         xsb[q:q + 1, own:own + 128] = W[4:5, 128 * q:128 * q + 128]
     fill_x(0)
-    start_all(xm(0))
-    start_all(xsm)
     for c in loads[11:]:
         c.wait()
 
@@ -407,19 +405,11 @@
 
         xms = xm(slot)
         cms = cm(slot)
-        for m in xms:
-            m.got()
-        use_x(slot)
-
-        @pl.when(k == 0)
-        def _():
-            for m in xsm:
-                m.got()
-            bed_x()
-            start_all(csm)
-
-        fill_c(slot)
-        start_all(cms)
+        for ms in am:
+            for m in ms:
+                m.sent()
+        start_all(xms)
+        pl.when(k == 0)(lambda: start_all(xsm))
 
         for p in range(PARTS):
             for m in am[p]:
@@ -432,6 +422,19 @@
             motion_part(p * size)
             start_all(bm[p])
 
+        for m in xms:
+            m.got()
+        use_x(slot)
+
+        @pl.when(k == 0)
+        def _():
+            for m in xsm:
+                m.got()
+            bed_x()
+            start_all(csm)
+
+        fill_c(slot)
+        start_all(cms)
         for m in cms:
             m.got()
         use_c(slot)
@@ -451,13 +454,10 @@
         @pl.when(k < STEPS - 1)
         def _():
             fill_x(nslot)
-            start_all(xm(nslot))
 
         for p in range(PARTS):
             for m in bm[p]:
                 m.got()
-            for m in am[p]:
-                m.sent()
             stress_part(p * size)
 
             @pl.when(k < STEPS - 1)

time: 52.9 us -> 55.7 us (1.053)
  the two profiles are of different devices: /device:TPU:6 before, /device:TPU:14 now
where the time goes in v5:
time: 55.7 us; the launch traced here: 55.5 us
  Pallas kernels  54.9 us (99%)
  between operations  0.64 us (1%)
    pallas_call x1, Pallas kernels, body(): pl.pallas_call(functools.partial(kernel, nx, ny), out_shape=[pltpu.VMEM(s...  53.8 us

profile of v5, /device:TPU:14, one launch (start us, length us, event | category | flops | bytes accessed | tf_op | source)
XLA Modules:
  0.0 55.5 jit_solution(15194029663718563262)
XLA Ops:
  0.6 53.8 %coupled.1 = (f32[3,2,96,128]{3,2,1,0:T(8,128)S(1)}, f32[6,2,96,128]{3,2,1,0:T(8,128)S(1)}, f32[24,1152]{1,0:T(8,128)S(1)}, f32[24,1152]{1,0:T(8,128)S(1)}, f32[24,1152]{1,0:T(8,128)S(1)}) custom-call(f32[3,2,96,128]{3,2,1,0:T(8,128)} %motion.1, f32[6,2,96,128]{3,2,1,0:T(8,128)} %stress.1, f32[2,96,128]{2,1,0:T(8,128)} %buoy.1, f32[2,96,128]{2,1,0:T(8,128)} %lame1.1, ...), custom_call_target="tpu_custom_call" | custom-call | tf_op jit(solution)/shard_map/coupled/pallas_call | solution.py:519
  54.5 1.0 %write_out.1 = (f32[3,2,96,128]{3,2,1,0:T(8,128)}, f32[6,2,96,128]{3,2,1,0:T(8,128)}, f32[16,1024]{1,0:T(8,128)}, f32[2,16,1024]{2,1,0:T(8,128)}) custom-call(f32[3,2,96,128]{3,2,1,0:T(8,128)S(1)} %get-tuple-element.9.V, f32[6,2,96,128]{3,2,1,0:T(8,128)S(1)} %get-tuple-element.10.S, f32[24,1152]{1,0:T(8,128)S(1)} %get-tuple-element.11.H, ...), custom_call_target="tpu_custom_call" | custom-call | tf_op jit(solution)/shard_map/write_out/pallas_call | solution.py:530

commit v6 on v4

--- a/solution.py
+++ b/solution.py
@@ -10,7 +10,7 @@
 RATIO = 8
 STEPS = 4
 NSUB = 4
-PARTS = 3
+PARTS = 2
 SOLID_STEP = 0.2
 WAVE_STEP = 0.1
 VISCOSITY = 0.05
@@ -401,13 +401,8 @@
             S[4, x, zs] = S[4, x, zs] + g * ((yp(vx, hu_v[1, x, zs]) - vx) + (vy_a - vy))
             S[5, x, zs] = S[5, x, zs] + g * ((zp(V, 0, x, z) - vy) + (yp(vz, hu_v[0, x, zs]) - vz))
 
-    def step(k, carry):
-        slot = lax.rem(k, 2)
-        nslot = lax.rem(k + 1, 2)
-
-        xms = xm(slot)
-        cms = cm(slot)
-        for m in xms:
+    def waves(k, slot):
+        for m in xm(slot):
             m.got()
         use_x(slot)
 
@@ -419,8 +414,27 @@
             start_all(csm)
 
         fill_c(slot)
-        start_all(cms)
-
+        start_all(cm(slot))
+        for m in cm(slot):
+            m.got()
+        use_c(slot)
+
+        @pl.when(k == 0)
+        def _():
+            for m in csm:
+                m.got()
+            ocean_setup()
+            mask_flow()
+
+        lift()
+        lax.fori_loop(0, NSUB, substep, 0)
+        average(slot)
+
+    def step(k, carry):
+        slot = lax.rem(k, 2)
+        nslot = lax.rem(k + 1, 2)
+
+        pl.when(k > 0)(lambda: waves(k, slot))
         for p in range(PARTS):
             for m in am[p]:
                 m.got()
@@ -432,25 +446,18 @@
             motion_part(p * size)
             start_all(bm[p])
 
-        for m in cms:
-            m.got()
-        use_c(slot)
-
-        @pl.when(k == 0)
-        def _():
-            for m in csm:
-                m.got()
-            ocean_setup()
-            mask_flow()
-
-        lift()
-        lax.fori_loop(0, NSUB, substep, 0)
-        last = k == STEPS - 1
-        pl.when(last)(lambda: average(slot))
+        pl.when(k == 0)(lambda: waves(k, slot))
 
         @pl.when(k < STEPS - 1)
         def _():
             fill_x(nslot)
+
+        for ms in bm:
+            for m in ms:
+                m.sent()
+
+        @pl.when(k < STEPS - 1)
+        def _():
             start_all(xm(nslot))
 
         for p in range(PARTS):
@@ -464,11 +471,7 @@
             def _():
                 start_all(am[p])
 
-        pl.when(jnp.logical_not(last))(lambda: average(slot))
-        for ms in bm:
-            for m in ms:
-                m.sent()
-        for m in xms + cms:
+        for m in xm(slot) + cm(slot):
             m.sent()
         lm(slot).sent()
         return carry

time: 52.9 us -> 54.1 us (1.023)
  the two profiles are of different devices: /device:TPU:6 before, /device:TPU:0 now
where the time goes in v6:
time: 54.1 us; the launch traced here: 54 us
  Pallas kernels  53.3 us (99%)
  between operations  0.64 us (1%)
    pallas_call x1, Pallas kernels, body(): pl.pallas_call(functools.partial(kernel, nx, ny), out_shape=[pltpu.VMEM(s...  52.3 us

profile of v6, /device:TPU:0, one launch (start us, length us, event | category | flops | bytes accessed | tf_op | source)
XLA Modules:
  0.0 54.0 jit_solution(17088228474978038557)
XLA Ops:
  0.6 52.3 %coupled.1 = (f32[3,2,96,128]{3,2,1,0:T(8,128)S(1)}, f32[6,2,96,128]{3,2,1,0:T(8,128)S(1)}, f32[24,1152]{1,0:T(8,128)S(1)}, f32[24,1152]{1,0:T(8,128)S(1)}, f32[24,1152]{1,0:T(8,128)S(1)}) custom-call(f32[3,2,96,128]{3,2,1,0:T(8,128)} %motion.1, f32[6,2,96,128]{3,2,1,0:T(8,128)} %stress.1, f32[2,96,128]{2,1,0:T(8,128)} %buoy.1, f32[2,96,128]{2,1,0:T(8,128)} %lame1.1, ...), custom_call_target="tpu_custom_call" | custom-call | tf_op jit(solution)/shard_map/coupled/pallas_call | solution.py:522
  52.9 1.0 %write_out.1 = (f32[3,2,96,128]{3,2,1,0:T(8,128)}, f32[6,2,96,128]{3,2,1,0:T(8,128)}, f32[16,1024]{1,0:T(8,128)}, f32[2,16,1024]{2,1,0:T(8,128)}) custom-call(f32[3,2,96,128]{3,2,1,0:T(8,128)S(1)} %get-tuple-element.9.V, f32[6,2,96,128]{3,2,1,0:T(8,128)S(1)} %get-tuple-element.10.S, f32[24,1152]{1,0:T(8,128)S(1)} %get-tuple-element.11.H, ...), custom_call_target="tpu_custom_call" | custom-call | tf_op jit(solution)/shard_map/write_out/pallas_call | solution.py:533
